TPU v7x, 32 devices: a whole 2x2x4 slice. The times are simulated.
32 devices in a mesh: src: 32 (over z, y, x, core), dst: 1.
Axes of the slice: x: 2, y: 2, z: 4, core: 2. Of those that a mesh axis runs over, the one named last changes fastest.
Arguments:
- out_density: float32 [16384], P('src'), may hold values from 0.008 to 0.08
- in_density: float32 [16384], P('dst'), may hold values from 0.008 to 0.08
- retention: float32 [16384], P('src'), may hold values from 0.15 to 0.75
- demand: float32 [16384], P('src'), may hold values from 0.5 to 4
- location: int32 [16384], replicated, may hold values from 0 to 16383
- scenario_blocks: int32 [32], replicated, may hold values from 0 to 127
Outputs:
- out_fitness: float32 [16384], P('src')
- in_fitness: float32 [16384], P('dst')
- levels: float32 [16384, 32], P('src', 'dst')
Inputs may be any that keep to these rules, and one draw needn't show every extreme that they name: `scenario_blocks`: scenario k extracts the 128 firms of block index b = scenario_blocks_k, firms 128 * b to 128 * b + 127. `location`: several firms may share a map cell, and some cells hold none.
All inputs are finite; a program needn't handle non-finite values.
Results may differ from a plain program's by a relative error of at most 0.0003.
Values sent between devices are 32-bit elements; how exact they have to be, the bound alone decides.
A program may use at most 64 MiB of HBM per device.

v0:
```python
import math
import jax
import jax.numpy as jnp
from jax import lax
from jax.sharding import PartitionSpec as P

SWEEPS = 2
ITERS = 2
EXTRACT = 128
MAP_SIDE = 256
RANGE = 18
far_weight = 0.015625


def on_device(out_density, in_density, retention, demand, location, scenario_blocks):
    rows_dev = out_density.shape[0]
    cols_dev = in_density.shape[0]
    firms = rows_dev * lax.axis_size("src")
    row_start = lax.axis_index("src") * rows_dev
    col_start = lax.axis_index("dst") * cols_dev
    height = math.gcd(rows_dev, 128)
    blocks = rows_dev // height
    col_ids = col_start + jnp.arange(cols_dev, dtype=jnp.int32)
    offsets = jnp.arange(blocks, dtype=jnp.int32) * height
    src_cells = lax.dynamic_slice_in_dim(location, row_start, rows_dev)
    dst_cells = lax.dynamic_slice_in_dim(location, col_start, cols_dev)
    src_row = src_cells // MAP_SIDE
    src_col = src_cells % MAP_SIDE
    dst_row = dst_cells // MAP_SIDE
    dst_col = dst_cells % MAP_SIDE
    out_fit = jnp.sqrt(out_density)
    in_fit = jnp.sqrt(in_density)

    def pair_weight(offset):
        row_ids = row_start + offset + jnp.arange(height, dtype=jnp.int32)
        row_gap = lax.dynamic_slice_in_dim(src_row, offset, height)[:, None] - dst_row[None, :]
        col_gap = lax.dynamic_slice_in_dim(src_col, offset, height)[:, None] - dst_col[None, :]
        nearby = row_gap * row_gap + col_gap * col_gap <= RANGE * RANGE
        affinity = jnp.where(nearby, 1.0, far_weight)
        return jnp.where(row_ids[:, None] != col_ids[None, :], affinity, 0.0)

    for sweep_no in range(SWEEPS):

        def row_part(offset):
            row_fit = lax.dynamic_slice_in_dim(out_fit, offset, height)
            weight = pair_weight(offset)
            ratios = weight * in_fit[None, :] / (1.0 + row_fit[:, None] * in_fit[None, :] * weight)
            return jnp.sum(ratios, axis=1)

        row_partial = lax.map(row_part, offsets).reshape(rows_dev)
        row_total = lax.psum(row_partial, "dst")
        out_fit = firms * out_density / row_total

        def col_part(running, offset):
            row_fit = lax.dynamic_slice_in_dim(out_fit, offset, height)
            weight = pair_weight(offset)
            ratios = weight * row_fit[:, None] / (1.0 + row_fit[:, None] * in_fit[None, :] * weight)
            return (running + jnp.sum(ratios, axis=0), None)

        col_partial, _ = lax.scan(col_part, jnp.zeros((cols_dev,), jnp.float32), offsets)
        col_total = lax.psum(col_partial, "src")
        in_fit = firms * in_density / col_total
    row_scale = retention / (firms * out_density)

    def coeff_block(offset):
        row_fit = lax.dynamic_slice_in_dim(out_fit, offset, height)
        scale_part = lax.dynamic_slice_in_dim(row_scale, offset, height)
        product = row_fit[:, None] * in_fit[None, :] * pair_weight(offset)
        chance = product / (1.0 + product)
        return chance * scale_part[:, None]

    coefficients = lax.map(coeff_block, offsets).reshape(rows_dev, cols_dev)
    scenarios = scenario_blocks.shape[0]
    portion = scenarios // lax.axis_size("dst")
    leading = lax.axis_index("dst") * portion
    firm_rows = row_start + jnp.arange(rows_dev, dtype=jnp.int32)
    retained = (firm_rows[:, None] // EXTRACT != scenario_blocks[None, :]).astype(jnp.float32)
    levels = retained * demand[:, None]
    for round_no in range(ITERS):
        every_row = lax.all_gather(levels, "src", axis=0, tiled=True)
        columns = lax.dynamic_slice_in_dim(every_row, col_start, cols_dev, 0)
        summed = lax.psum(
            jnp.dot(
                coefficients,
                columns,
                preferred_element_type=jnp.float32,
                precision=lax.Precision.HIGHEST,
            ),
            "dst",
        )
        levels = retained * (demand[:, None] + summed)
    result = lax.dynamic_slice_in_dim(levels, leading, portion, 1)
    return (out_fit, in_fit, result)


def solution(mesh):
    in_specs = (P("src"), P("dst"), P("src"), P("src"), P(), P())
    out_specs = (P("src"), P("dst"), P("src", "dst"))
    return jax.shard_map(
        on_device, mesh=mesh, in_specs=in_specs, out_specs=out_specs, check_vma=False
    )
```

profile of v0, /device:TPU:0, one launch (start us, length us, event | category | flops | bytes accessed | tf_op | source)
XLA Modules:
  0.0 580.2 jit_solution(1393125838560426272)
XLA Ops:
  7.3 0.9 add_select_fusion
  8.2 0.8 add_select_fusion.3
  8.9 0.9 sqrt.6
  9.8 0.7 sqrt.7
  10.5 33.4 %while.55 = (s32[]{:T(128)}, f32[4,128]{1,0:T(4,128)S(1)}, s32[4]{0:T(128)S(1)}, s32[]{:T(128)}, s32[512]{0:T(512)S(1)}, /*index=5*/s32[16384]{0:T(1024)S(1)}, s...) while((s32[]{:T(128)}, f32[4,128]{1,0:T(4,128)S(1)}, ...), condition=%wide.region_2.3_spmd.clone, body=%wide.region_0.2_spmd.clone.sunk | while | flops 31457284 | bytes 203979 | solution.py:50
  10.5 0.6 dynamic_slice.120
  13.9 4.9 fusion.33
  18.9 0.6 dynamic_slice.120
  22.3 4.9 fusion.33
  30.6 4.9 fusion.33
  35.6 0.6 dynamic_slice.120
  39.0 4.9 fusion.33
  43.9 0.7 bitcast_divide_fusion.1
  44.6 34.3 %while.58 = (s32[]{:T(128)}, f32[16384]{0:T(1024)S(1)}, s32[4]{0:T(128)S(1)}, s32[]{:T(128)}, s32[512]{0:T(512)S(1)}, /*index=5*/s32[16384]{0:T(1024)S(1)}, s32[...) while((s32[]{:T(128)}, f32[16384]{0:T(1024)S(1)}, ...), condition=%wide.region_5.6_spmd.clone, body=%wide.region_3.5_spmd.clone.sunk | while | flops 31473796 | bytes 464593 | solution.py:60
  44.6 0.6 dynamic_slice.133
  48.0 5.1 fusion.36
  53.2 0.6 dynamic_slice.133
  56.6 5.1 fusion.36
  61.8 0.6 dynamic_slice.133
  65.2 5.1 fusion.36
  73.8 5.1 fusion.36
  79.0 0.6 copy-done.1
  79.7 120.3 %all-reduce.3.cloned.1.call-done = f32[16384]{0:T(1024)} async-done(((f32[16384]{0:T(1024)}), f32[16384]{0:T(1024)}) %all-reduce.3.cloned.1.call-update) | async-done | bytes 65552 | tf_op jit(solution)/shard_map/psum | solution.py:61
  200.0 0.9 multiply_divide_fusion.1
  200.9 33.4 %while.56 = (s32[]{:T(128)}, f32[4,128]{1,0:T(4,128)S(1)}, s32[4]{0:T(128)S(1)}, s32[]{:T(128)}, s32[512]{0:T(512)S(1)}, /*index=5*/s32[16384]{0:T(1024)S(1)}, s...) while((s32[]{:T(128)}, f32[4,128]{1,0:T(4,128)S(1)}, ...), condition=%wide.region_9.10_spmd.clone, body=%wide.region_7.9_spmd.clone.sunk | while | flops 31457284 | bytes 203979 | solution.py:50
  204.3 4.9 fusion.34
  212.7 4.9 fusion.34
  221.0 4.9 fusion.34
  229.4 4.9 fusion.34
  234.3 0.7 multiply_divide_fusion.2
  235.0 34.3 %while.59 = (s32[]{:T(128)}, f32[16384]{0:T(1024)S(1)}, s32[4]{0:T(128)S(1)}, s32[]{:T(128)}, s32[512]{0:T(512)S(1)}, /*index=5*/s32[16384]{0:T(1024)S(1)}, s32[...) while((s32[]{:T(128)}, f32[16384]{0:T(1024)S(1)}, ...), condition=%wide.region_12.13_spmd.clone, body=%wide.region_10.12_spmd.clone.sunk | while | flops 31473796 | bytes 464593 | solution.py:60
  238.4 5.1 fusion.37
  247.0 5.1 fusion.37
  255.6 5.1 fusion.37
  264.2 5.1 fusion.37
  269.4 0.6 copy-done.2
  270.1 0.7 compare_select_fusion
  271.0 117.5 %all-reduce.5.cloned.1.call-done = f32[16384]{0:T(1024)} async-done(((f32[16384]{0:T(1024)}), f32[16384]{0:T(1024)}) %all-reduce.5.cloned.1.call-update) | async-done | bytes 65552 | tf_op jit(solution)/shard_map/psum | solution.py:61
  388.5 0.9 multiply_divide_fusion
  389.4 39.0 %while.57 = (s32[]{:T(128)}, f32[4,128,16384]{2,1,0:T(8,128)}, s32[4]{0:T(128)S(1)}, f32[512]{0:T(512)S(1)}, f32[16384]{0:T(1024)S(1)}, /*index=5*/s32[]{:T(128)...) while((s32[]{:T(128)}, f32[4,128,16384]{2,1,0:T(8,128)}, ...), condition=%wide.region_15.16_spmd.clone, body=%wide.region_14.15_spmd.clone.sunk | while | flops 29360260 | bytes 8593107 | solution.py:72
  392.9 6.3 %fusion.35 = f32[4,128,16384]{2,1,0:T(8,128)} fusion(f32[4,128,16384]{2,1,0:T(8,128)} %get-tuple-element.1026, s32[]{:T(128)} %get-tuple-element.1025, f32[128]{0:T(128)S(1)} %dynamic_slice.129, s32[16384]{0:T(1024)S(1)} %get-tuple-element.1048, s32[128]{0:T(128)S(1)} %dynamic_slice.130, s32[16384]{0:T(1024)S(1)} %get-tuple-element.1046, ...), kind=kLoop, calls=%fused_computation.17.clone.1 | loop fusion | flops 29360128 | bytes 8588288 | tf_op jit(solution)/shard_map/while/body/jit(dynamic_update_index_in_dim)/dynamic_update_slice | solution.py:72
  402.6 6.2 %fusion.35 = f32[4,128,16384]{2,1,0:T(8,128)} fusion(f32[4,128,16384]{2,1,0:T(8,128)} %get-tuple-element.1026, s32[]{:T(128)} %get-tuple-element.1025, f32[128]{0:T(128)S(1)} %dynamic_slice.129, s32[16384]{0:T(1024)S(1)} %get-tuple-element.1048, s32[128]{0:T(128)S(1)} %dynamic_slice.130, s32[16384]{0:T(1024)S(1)} %get-tuple-element.1046, ...), kind=kLoop, calls=%fused_computation.17.clone.1 | loop fusion | flops 29360128 | bytes 8588288 | tf_op jit(solution)/shard_map/while/body/jit(dynamic_update_index_in_dim)/dynamic_update_slice | solution.py:72
  412.4 6.3 %fusion.35 = f32[4,128,16384]{2,1,0:T(8,128)} fusion(f32[4,128,16384]{2,1,0:T(8,128)} %get-tuple-element.1026, s32[]{:T(128)} %get-tuple-element.1025, f32[128]{0:T(128)S(1)} %dynamic_slice.129, s32[16384]{0:T(1024)S(1)} %get-tuple-element.1048, s32[128]{0:T(128)S(1)} %dynamic_slice.130, s32[16384]{0:T(1024)S(1)} %get-tuple-element.1046, ...), kind=kLoop, calls=%fused_computation.17.clone.1 | loop fusion | flops 29360128 | bytes 8588288 | tf_op jit(solution)/shard_map/while/body/jit(dynamic_update_index_in_dim)/dynamic_update_slice | solution.py:72
  422.1 6.2 %fusion.35 = f32[4,128,16384]{2,1,0:T(8,128)} fusion(f32[4,128,16384]{2,1,0:T(8,128)} %get-tuple-element.1026, s32[]{:T(128)} %get-tuple-element.1025, f32[128]{0:T(128)S(1)} %dynamic_slice.129, s32[16384]{0:T(1024)S(1)} %get-tuple-element.1048, s32[128]{0:T(128)S(1)} %dynamic_slice.130, s32[16384]{0:T(1024)S(1)} %get-tuple-element.1046, ...), kind=kLoop, calls=%fused_computation.17.clone.1 | loop fusion | flops 29360128 | bytes 8588288 | tf_op jit(solution)/shard_map/while/body/jit(dynamic_update_index_in_dim)/dynamic_update_slice | solution.py:72
  428.3 20.0 %all-gather.3.cloned.1.call-done = f32[16384,32]{0,1:T(8,128)} async-done(((f32[512,32]{0,1:T(8,128)}), f32[16384,32]{0,1:T(8,128)}) %all-gather.3.cloned.1.call-update) | async-done | bytes 2097168 | tf_op jit(solution)/shard_map/all_gather | solution.py:80
  448.4 35.0 %fusion.17 = f32[512,32]{0,1:T(8,128)} fusion(f32[512,16384]{1,0:T(8,128)} %bitcast.30, f32[16384,32]{0,1:T(8,128)} %all-gather.3.cloned.1.call-done, f32[512]{0:T(512)S(1)} %copy-done.4, s32[512]{0:T(512)S(1)} %add_select_fusion.2, s32[32]{0:T(128)S(1)} %copy-done.5), kind=kOutput, calls=%fused_computation.36 | convolution fusion | flops 3221274624 | bytes 35721344 | tf_op jit(solution)/shard_map/dot_general | solution.py:83
  483.4 55.3 %all-gather.5.cloned.1.call-done = f32[16384,32]{0,1:T(8,128)} async-done(((f32[512,32]{0,1:T(8,128)}), f32[16384,32]{0,1:T(8,128)}) %all-gather.5.cloned.1.call-update) | async-done | bytes 2097168 | tf_op jit(solution)/shard_map/all_gather | solution.py:80
  538.7 35.0 %fusion.16 = f32[512,32]{0,1:T(8,128)} fusion(f32[512,16384]{1,0:T(8,128)} %bitcast.31, f32[16384,32]{0,1:T(8,128)} %all-gather.5.cloned.1.call-done, f32[512]{0:T(512)S(1)} %copy-done.4, s32[512]{0:T(512)S(1)} %add_select_fusion.2, s32[32]{0:T(128)S(1)} %copy-done.5), kind=kOutput, calls=%fused_computation.34 | convolution fusion | flops 3221274624 | bytes 35721344 | tf_op jit(solution)/shard_map/dot_general | solution.py:83
  (141 shorter events, 14.0 us)
Async XLA Ops:
  7.2 381.3 %copy-start.3 = (f32[16384]{0:T(1024)S(1)}, f32[16384]{0:T(1024)}, u32[]{:S(2)}) copy-start(f32[16384]{0:T(1024)} %param.17) | copy-start | bytes 196612
  7.2 262.9 %copy-start.4 = (f32[512]{0:T(512)S(1)}, f32[512]{0:T(512)}, u32[]{:S(2)}) copy-start(f32[512]{0:T(512)} %param.19) | copy-start | bytes 6148
  7.2 262.9 %copy-start.5 = (s32[32]{0:T(128)S(1)}, s32[32]{0:T(128)}, u32[]{:S(2)}) copy-start(s32[32]{0:T(128)} %param.21) | copy-start | bytes 388
  7.2 192.8 %all-reduce.3.cloned.1.call-start = ((), (), s32[]{:S(2)}) async-start(), calls=%async_computation | async-start | bytes 131072 | tf_op jit(solution)/shard_map/psum | solution.py:61
  78.9 0.6 copy-start.1
  79.6 308.9 %all-reduce.5.cloned.1.call-start = ((), (), s32[]{:S(2)}) async-start(), calls=%async_computation.1 | async-start | bytes 131072 | tf_op jit(solution)/shard_map/psum | solution.py:61
  269.4 0.6 copy-start.2
  270.0 178.4 %all-gather.3.cloned.1.call-start = ((), (), s32[]{:S(2)}) async-start(), calls=%async_computation.2 | async-start | bytes 2162688 | tf_op jit(solution)/shard_map/all_gather | solution.py:80
  270.8 267.9 %all-gather.5.cloned.1.call-start = ((), (), s32[]{:S(2)}) async-start(), calls=%async_computation.3 | async-start | bytes 2162688 | tf_op jit(solution)/shard_map/all_gather | solution.py:80
  428.3 55.1 %copy-start = (f32[16384]{0:T(1024)}, f32[16384]{0:T(1024)S(1)}, u32[]{:S(2)}) copy-start(f32[16384]{0:T(1024)S(1)} %get-tuple-element.1067) | copy-start | bytes 196612
  428.3 55.1 %copy-start.6 = (f32[512]{0:T(512)}, f32[512]{0:T(512)S(1)}, u32[]{:S(2)}) copy-start(f32[512]{0:T(512)S(1)} %get-tuple-element.1081) | copy-start | bytes 6148
Sparse Core Ops, SparseCore 0:
  79.7 120.2 all-reduce.2
  270.1 118.3 all-reduce.4
  391.4 56.9 all-gather.2
  483.5 55.1 all-gather.4
where the time goes:
time: 581 us; the launch traced here: 580 us
  waiting for transfers between devices  313 us (54%)
  other arithmetic  111 us (19%)
  matrix products  70 us (12%)
  loops' own time  52.4 us (9%)
  local copies, waits for them, and re-layouts  19.6 us (3%)
  between operations  13.9 us (2%)
    psum x2, waiting for transfers between devices, on_device(): col_total = lax.psum(col_partial, 'src')  238 us
    all_gather x2, waiting for transfers between devices, on_device(): every_row = lax.all_gather(levels, 'src', axis=0, tiled=True)  75.3 us
    dot_general x2, matrix products, on_device(): jnp.dot(coefficients, columns, preferred_element_type=jnp.float32, precis...  70 us
    reduce_sum x8, other arithmetic, col_part(): return (running + jnp.sum(ratios, axis=0), None)  40.9 us
    reduce_sum x8, other arithmetic, row_part(): return jnp.sum(ratios, axis=1)  39.1 us
    dynamic_update_slice x4, other arithmetic, on_device(): coefficients = lax.map(coeff_block, offsets).reshape(rows_dev, cols_dev)  25 us
    another operation x2, loops' own time, on_device(): lax.scan(col_part, jnp.zeros((cols_dev,), jnp.float32), offsets)  21.1 us
    another operation x2, loops' own time, on_device(): row_partial = lax.map(row_part, offsets).reshape(rows_dev)  20.9 us
  transfers between devices with their start and end apart: 4, of which 4 were waited for; matrix products, arithmetic and copies ran while one was open for 5% of the time, Pallas kernels for 0%

commit v1 on v0

--- a/solution.py
+++ b/solution.py
@@ -58,7 +58,7 @@
             return (running + jnp.sum(ratios, axis=0), None)
 
         col_partial, _ = lax.scan(col_part, jnp.zeros((cols_dev,), jnp.float32), offsets)
-        col_total = lax.psum(col_partial, "src")
+        col_total = jnp.sum(lax.all_gather(col_partial, "src"), 0)
         in_fit = firms * in_density / col_total
     row_scale = retention / (firms * out_density)
 

time: 581 us -> 455 us (0.78)
  waiting for transfers between devices: 313 us -> 186 us
    psum x2 -> x0, waiting for transfers between devices: 238 us -> none  [on_device(): col_total = lax.psum(col_partial, 'src')]
    all_gather x0 -> x2, waiting for transfers between devices: none -> 114 us  [on_device(): col_total = jnp.sum(lax.all_gather(col_partial, 'src'), 0)]
  transfers between devices with their start and end apart: 4 -> 4, of which waited for: 4 -> 4; matrix products, arithmetic and copies ran while one was open for 5% -> 7% of each run, Pallas kernels for 0% -> 0%
where the time goes in v1:
time: 455 us; the launch traced here: 454 us
  waiting for transfers between devices  186 us (41%)
  other arithmetic  109 us (24%)
  matrix products  70 us (15%)
  loops' own time  52.4 us (12%)
  local copies, waits for them, and re-layouts  23.1 us (5%)
  between operations  14 us (3%)
    all_gather x2, waiting for transfers between devices, on_device(): col_total = jnp.sum(lax.all_gather(col_partial, 'src'), 0)  114 us
    all_gather x2, waiting for transfers between devices, on_device(): every_row = lax.all_gather(levels, 'src', axis=0, tiled=True)  72.2 us
    dot_general x2, matrix products, on_device(): jnp.dot(coefficients, columns, preferred_element_type=jnp.float32, precis...  70 us
    reduce_sum x8, other arithmetic, col_part(): return (running + jnp.sum(ratios, axis=0), None)  40.8 us
    reduce_sum x8, other arithmetic, row_part(): return jnp.sum(ratios, axis=1)  39.1 us
    dynamic_update_slice x4, other arithmetic, on_device(): coefficients = lax.map(coeff_block, offsets).reshape(rows_dev, cols_dev)  25 us
    another operation x2, loops' own time, on_device(): lax.scan(col_part, jnp.zeros((cols_dev,), jnp.float32), offsets)  21.1 us
    another operation x2, loops' own time, on_device(): row_partial = lax.map(row_part, offsets).reshape(rows_dev)  20.9 us
  transfers between devices with their start and end apart: 4, of which 4 were waited for; matrix products, arithmetic and copies ran while one was open for 7% of the time, Pallas kernels for 0%

profile of v1, /device:TPU:0, one launch (start us, length us, event | category | flops | bytes accessed | tf_op | source)
XLA Modules:
  0.0 454.3 jit_solution(4716506894703659780)
XLA Ops:
  7.3 0.9 add_select_fusion
  8.2 0.8 add_select_fusion.3
  9.0 0.9 sqrt.6
  9.8 0.7 sqrt.7
  10.5 33.4 %while.55 = (s32[]{:T(128)}, f32[4,128]{1,0:T(4,128)S(1)}, s32[4]{0:T(128)S(1)}, s32[]{:T(128)}, s32[512]{0:T(512)S(1)}, /*index=5*/s32[16384]{0:T(1024)S(1)}, s...) while((s32[]{:T(128)}, f32[4,128]{1,0:T(4,128)S(1)}, ...), condition=%wide.region_2.3_spmd.clone, body=%wide.region_0.2_spmd.clone.sunk | while | flops 31457284 | bytes 203979 | solution.py:50
  10.5 0.6 dynamic_slice.120
  13.9 4.9 %fusion.33 = f32[128]{0:T(128)S(1)} fusion(f32[128]{0:T(128)S(1)} %dynamic_slice.121, f32[16384]{0:T(1024)S(1)} %get-tuple-element.889, s32[16384]{0:T(1024)S(1)} %get-tuple-element.888, s32[128]{0:T(128)S(1)} %dynamic_slice.122, s32[16384]{0:T(1024)S(1)} %get-tuple-element.886, s32[128]{0:T(128)S(1)} %dynamic_slice.123, s32[128]{0:T(128)S(1)} %iota_add_fusion.11), kind=kLoop, calls=%fused_computation.8.clone.1 | loop fusion | flops 31457152 | bytes 199168 | tf_op jit(solution)/shard_map/while/body/eval_jaxpr/reduce_sum | solution.py:48
  22.3 4.9 %fusion.33 = f32[128]{0:T(128)S(1)} fusion(f32[128]{0:T(128)S(1)} %dynamic_slice.121, f32[16384]{0:T(1024)S(1)} %get-tuple-element.889, s32[16384]{0:T(1024)S(1)} %get-tuple-element.888, s32[128]{0:T(128)S(1)} %dynamic_slice.122, s32[16384]{0:T(1024)S(1)} %get-tuple-element.886, s32[128]{0:T(128)S(1)} %dynamic_slice.123, s32[128]{0:T(128)S(1)} %iota_add_fusion.11), kind=kLoop, calls=%fused_computation.8.clone.1 | loop fusion | flops 31457152 | bytes 199168 | tf_op jit(solution)/shard_map/while/body/eval_jaxpr/reduce_sum | solution.py:48
  27.2 0.6 dynamic_slice.120
  30.6 4.9 %fusion.33 = f32[128]{0:T(128)S(1)} fusion(f32[128]{0:T(128)S(1)} %dynamic_slice.121, f32[16384]{0:T(1024)S(1)} %get-tuple-element.889, s32[16384]{0:T(1024)S(1)} %get-tuple-element.888, s32[128]{0:T(128)S(1)} %dynamic_slice.122, s32[16384]{0:T(1024)S(1)} %get-tuple-element.886, s32[128]{0:T(128)S(1)} %dynamic_slice.123, s32[128]{0:T(128)S(1)} %iota_add_fusion.11), kind=kLoop, calls=%fused_computation.8.clone.1 | loop fusion | flops 31457152 | bytes 199168 | tf_op jit(solution)/shard_map/while/body/eval_jaxpr/reduce_sum | solution.py:48
  35.6 0.6 dynamic_slice.120
  39.0 4.9 %fusion.33 = f32[128]{0:T(128)S(1)} fusion(f32[128]{0:T(128)S(1)} %dynamic_slice.121, f32[16384]{0:T(1024)S(1)} %get-tuple-element.889, s32[16384]{0:T(1024)S(1)} %get-tuple-element.888, s32[128]{0:T(128)S(1)} %dynamic_slice.122, s32[16384]{0:T(1024)S(1)} %get-tuple-element.886, s32[128]{0:T(128)S(1)} %dynamic_slice.123, s32[128]{0:T(128)S(1)} %iota_add_fusion.11), kind=kLoop, calls=%fused_computation.8.clone.1 | loop fusion | flops 31457152 | bytes 199168 | tf_op jit(solution)/shard_map/while/body/eval_jaxpr/reduce_sum | solution.py:48
  43.9 0.7 bitcast_divide_fusion.1
  44.6 34.3 %while.58 = (s32[]{:T(128)}, f32[16384]{0:T(1024)S(1)}, s32[4]{0:T(128)S(1)}, s32[]{:T(128)}, s32[512]{0:T(512)S(1)}, /*index=5*/s32[16384]{0:T(1024)S(1)}, s32[...) while((s32[]{:T(128)}, f32[16384]{0:T(1024)S(1)}, ...), condition=%wide.region_5.6_spmd.clone, body=%wide.region_3.5_spmd.clone.sunk | while | flops 31473796 | bytes 464593 | solution.py:60
  44.6 0.6 dynamic_slice.133
  48.0 5.1 %fusion.36 = f32[16384]{0:T(1024)S(1)} fusion(f32[16384]{0:T(1024)S(1)} %get-tuple-element.929, f32[128]{0:T(128)S(1)} %dynamic_slice.134, s32[16384]{0:T(1024)S(1)} %get-tuple-element.927, s32[128]{0:T(128)S(1)} %dynamic_slice.135, s32[16384]{0:T(1024)S(1)} %get-tuple-element.925, s32[128]{0:T(128)S(1)} %dynamic_slice.136, s32[128]{0:T(128)S(1)} %iota_add_fusion.14), kind=kLoop, calls=%fused_computation.24.clone.1 | loop fusion | flops 31440896 | bytes 264192 | tf_op jit(solution)/shard_map/while/body/eval_jaxpr/reduce_sum | solution.py:58
  53.2 0.6 dynamic_slice.133
  56.6 5.1 %fusion.36 = f32[16384]{0:T(1024)S(1)} fusion(f32[16384]{0:T(1024)S(1)} %get-tuple-element.929, f32[128]{0:T(128)S(1)} %dynamic_slice.134, s32[16384]{0:T(1024)S(1)} %get-tuple-element.927, s32[128]{0:T(128)S(1)} %dynamic_slice.135, s32[16384]{0:T(1024)S(1)} %get-tuple-element.925, s32[128]{0:T(128)S(1)} %dynamic_slice.136, s32[128]{0:T(128)S(1)} %iota_add_fusion.14), kind=kLoop, calls=%fused_computation.24.clone.1 | loop fusion | flops 31440896 | bytes 264192 | tf_op jit(solution)/shard_map/while/body/eval_jaxpr/reduce_sum | solution.py:58
  61.7 0.6 dynamic_slice.133
  65.2 5.1 %fusion.36 = f32[16384]{0:T(1024)S(1)} fusion(f32[16384]{0:T(1024)S(1)} %get-tuple-element.929, f32[128]{0:T(128)S(1)} %dynamic_slice.134, s32[16384]{0:T(1024)S(1)} %get-tuple-element.927, s32[128]{0:T(128)S(1)} %dynamic_slice.135, s32[16384]{0:T(1024)S(1)} %get-tuple-element.925, s32[128]{0:T(128)S(1)} %dynamic_slice.136, s32[128]{0:T(128)S(1)} %iota_add_fusion.14), kind=kLoop, calls=%fused_computation.24.clone.1 | loop fusion | flops 31440896 | bytes 264192 | tf_op jit(solution)/shard_map/while/body/eval_jaxpr/reduce_sum | solution.py:58
  70.3 0.6 dynamic_slice.133
  73.7 5.1 %fusion.36 = f32[16384]{0:T(1024)S(1)} fusion(f32[16384]{0:T(1024)S(1)} %get-tuple-element.929, f32[128]{0:T(128)S(1)} %dynamic_slice.134, s32[16384]{0:T(1024)S(1)} %get-tuple-element.927, s32[128]{0:T(128)S(1)} %dynamic_slice.135, s32[16384]{0:T(1024)S(1)} %get-tuple-element.925, s32[128]{0:T(128)S(1)} %dynamic_slice.136, s32[128]{0:T(128)S(1)} %iota_add_fusion.14), kind=kLoop, calls=%fused_computation.24.clone.1 | loop fusion | flops 31440896 | bytes 264192 | tf_op jit(solution)/shard_map/while/body/eval_jaxpr/reduce_sum | solution.py:58
  78.9 0.6 copy-done.1
  79.6 59.2 %all-gather.11.cloned.1.call-done = f32[524288]{0:T(1024)} async-done(((f32[16384]{0:T(1024)}), f32[524288]{0:T(1024)}) %all-gather.11.cloned.1.call-update) | async-done | bytes 2097168 | tf_op jit(solution)/shard_map/all_gather | solution.py:61
  138.7 1.7 reshape.326
  140.8 33.4 %while.56 = (s32[]{:T(128)}, f32[4,128]{1,0:T(4,128)S(1)}, s32[4]{0:T(128)S(1)}, s32[]{:T(128)}, s32[512]{0:T(512)S(1)}, /*index=5*/s32[16384]{0:T(1024)S(1)}, s...) while((s32[]{:T(128)}, f32[4,128]{1,0:T(4,128)S(1)}, ...), condition=%wide.region_9.10_spmd.clone, body=%wide.region_7.9_spmd.clone.sunk | while | flops 31457284 | bytes 203979 | solution.py:50
  144.2 4.9 %fusion.34 = f32[128]{0:T(128)S(1)} fusion(f32[128]{0:T(128)S(1)} %dynamic_slice.125, f32[16384]{0:T(1024)S(1)} %get-tuple-element.967, s32[16384]{0:T(1024)S(1)} %get-tuple-element.966, s32[128]{0:T(128)S(1)} %dynamic_slice.126, s32[16384]{0:T(1024)S(1)} %get-tuple-element.964, s32[128]{0:T(128)S(1)} %dynamic_slice.127, s32[128]{0:T(128)S(1)} %iota_add_fusion.12), kind=kLoop, calls=%fused_computation.13.clone.1 | loop fusion | flops 31457152 | bytes 199168 | tf_op jit(solution)/shard_map/while/body/eval_jaxpr/reduce_sum | solution.py:48
  152.5 4.9 %fusion.34 = f32[128]{0:T(128)S(1)} fusion(f32[128]{0:T(128)S(1)} %dynamic_slice.125, f32[16384]{0:T(1024)S(1)} %get-tuple-element.967, s32[16384]{0:T(1024)S(1)} %get-tuple-element.966, s32[128]{0:T(128)S(1)} %dynamic_slice.126, s32[16384]{0:T(1024)S(1)} %get-tuple-element.964, s32[128]{0:T(128)S(1)} %dynamic_slice.127, s32[128]{0:T(128)S(1)} %iota_add_fusion.12), kind=kLoop, calls=%fused_computation.13.clone.1 | loop fusion | flops 31457152 | bytes 199168 | tf_op jit(solution)/shard_map/while/body/eval_jaxpr/reduce_sum | solution.py:48
  160.9 4.9 %fusion.34 = f32[128]{0:T(128)S(1)} fusion(f32[128]{0:T(128)S(1)} %dynamic_slice.125, f32[16384]{0:T(1024)S(1)} %get-tuple-element.967, s32[16384]{0:T(1024)S(1)} %get-tuple-element.966, s32[128]{0:T(128)S(1)} %dynamic_slice.126, s32[16384]{0:T(1024)S(1)} %get-tuple-element.964, s32[128]{0:T(128)S(1)} %dynamic_slice.127, s32[128]{0:T(128)S(1)} %iota_add_fusion.12), kind=kLoop, calls=%fused_computation.13.clone.1 | loop fusion | flops 31457152 | bytes 199168 | tf_op jit(solution)/shard_map/while/body/eval_jaxpr/reduce_sum | solution.py:48
  169.2 4.9 %fusion.34 = f32[128]{0:T(128)S(1)} fusion(f32[128]{0:T(128)S(1)} %dynamic_slice.125, f32[16384]{0:T(1024)S(1)} %get-tuple-element.967, s32[16384]{0:T(1024)S(1)} %get-tuple-element.966, s32[128]{0:T(128)S(1)} %dynamic_slice.126, s32[16384]{0:T(1024)S(1)} %get-tuple-element.964, s32[128]{0:T(128)S(1)} %dynamic_slice.127, s32[128]{0:T(128)S(1)} %iota_add_fusion.12), kind=kLoop, calls=%fused_computation.13.clone.1 | loop fusion | flops 31457152 | bytes 199168 | tf_op jit(solution)/shard_map/while/body/eval_jaxpr/reduce_sum | solution.py:48
  174.2 34.3 %while.59 = (s32[]{:T(128)}, f32[16384]{0:T(1024)S(1)}, s32[4]{0:T(128)S(1)}, s32[]{:T(128)}, s32[512]{0:T(512)S(1)}, /*index=5*/s32[16384]{0:T(1024)S(1)}, s32[...) while((s32[]{:T(128)}, f32[16384]{0:T(1024)S(1)}, ...), condition=%wide.region_12.13_spmd.clone, body=%wide.region_10.12_spmd.clone.sunk | while | flops 31473796 | bytes 464593 | solution.py:60
  177.6 5.1 %fusion.37 = f32[16384]{0:T(1024)S(1)} fusion(f32[16384]{0:T(1024)S(1)} %get-tuple-element.1007, f32[128]{0:T(128)S(1)} %dynamic_slice.138, s32[16384]{0:T(1024)S(1)} %get-tuple-element.1005, s32[128]{0:T(128)S(1)} %dynamic_slice.139, s32[16384]{0:T(1024)S(1)} %get-tuple-element.1003, s32[128]{0:T(128)S(1)} %dynamic_slice.140, s32[128]{0:T(128)S(1)} %iota_add_fusion.15), kind=kLoop, calls=%fused_computation.30.clone.1 | loop fusion | flops 31440896 | bytes 264192 | tf_op jit(solution)/shard_map/while/body/eval_jaxpr/reduce_sum | solution.py:58
  186.2 5.1 %fusion.37 = f32[16384]{0:T(1024)S(1)} fusion(f32[16384]{0:T(1024)S(1)} %get-tuple-element.1007, f32[128]{0:T(128)S(1)} %dynamic_slice.138, s32[16384]{0:T(1024)S(1)} %get-tuple-element.1005, s32[128]{0:T(128)S(1)} %dynamic_slice.139, s32[16384]{0:T(1024)S(1)} %get-tuple-element.1003, s32[128]{0:T(128)S(1)} %dynamic_slice.140, s32[128]{0:T(128)S(1)} %iota_add_fusion.15), kind=kLoop, calls=%fused_computation.30.clone.1 | loop fusion | flops 31440896 | bytes 264192 | tf_op jit(solution)/shard_map/while/body/eval_jaxpr/reduce_sum | solution.py:58
  194.8 5.1 %fusion.37 = f32[16384]{0:T(1024)S(1)} fusion(f32[16384]{0:T(1024)S(1)} %get-tuple-element.1007, f32[128]{0:T(128)S(1)} %dynamic_slice.138, s32[16384]{0:T(1024)S(1)} %get-tuple-element.1005, s32[128]{0:T(128)S(1)} %dynamic_slice.139, s32[16384]{0:T(1024)S(1)} %get-tuple-element.1003, s32[128]{0:T(128)S(1)} %dynamic_slice.140, s32[128]{0:T(128)S(1)} %iota_add_fusion.15), kind=kLoop, calls=%fused_computation.30.clone.1 | loop fusion | flops 31440896 | bytes 264192 | tf_op jit(solution)/shard_map/while/body/eval_jaxpr/reduce_sum | solution.py:58
  203.3 5.1 %fusion.37 = f32[16384]{0:T(1024)S(1)} fusion(f32[16384]{0:T(1024)S(1)} %get-tuple-element.1007, f32[128]{0:T(128)S(1)} %dynamic_slice.138, s32[16384]{0:T(1024)S(1)} %get-tuple-element.1005, s32[128]{0:T(128)S(1)} %dynamic_slice.139, s32[16384]{0:T(1024)S(1)} %get-tuple-element.1003, s32[128]{0:T(128)S(1)} %dynamic_slice.140, s32[128]{0:T(128)S(1)} %iota_add_fusion.15), kind=kLoop, calls=%fused_computation.30.clone.1 | loop fusion | flops 31440896 | bytes 264192 | tf_op jit(solution)/shard_map/while/body/eval_jaxpr/reduce_sum | solution.py:58
  208.5 0.6 copy-done.2
  209.2 0.7 compare_select_fusion
  210.2 54.3 %all-gather.13.cloned.1.call-done = f32[524288]{0:T(1024)} async-done(((f32[16384]{0:T(1024)}), f32[524288]{0:T(1024)}) %all-gather.13.cloned.1.call-update) | async-done | bytes 2097168 | tf_op jit(solution)/shard_map/all_gather | solution.py:61
  264.5 1.7 reshape.327
  266.5 38.9 %while.57 = (s32[]{:T(128)}, f32[4,128,16384]{2,1,0:T(8,128)}, s32[4]{0:T(128)S(1)}, f32[512]{0:T(512)S(1)}, f32[16384]{0:T(1024)S(1)}, /*index=5*/s32[]{:T(128)...) while((s32[]{:T(128)}, f32[4,128,16384]{2,1,0:T(8,128)}, ...), condition=%wide.region_15.16_spmd.clone, body=%wide.region_14.15_spmd.clone.sunk | while | flops 29360260 | bytes 8593107 | solution.py:72
  270.0 6.3 %fusion.35 = f32[4,128,16384]{2,1,0:T(8,128)} fusion(f32[4,128,16384]{2,1,0:T(8,128)} %get-tuple-element.1026, s32[]{:T(128)} %get-tuple-element.1025, f32[128]{0:T(128)S(1)} %dynamic_slice.129, s32[16384]{0:T(1024)S(1)} %get-tuple-element.1048, s32[128]{0:T(128)S(1)} %dynamic_slice.130, s32[16384]{0:T(1024)S(1)} %get-tuple-element.1046, ...), kind=kLoop, calls=%fused_computation.17.clone.1 | loop fusion | flops 29360128 | bytes 8588288 | tf_op jit(solution)/shard_map/while/body/jit(dynamic_update_index_in_dim)/dynamic_update_slice | solution.py:72
  279.8 6.2 %fusion.35 = f32[4,128,16384]{2,1,0:T(8,128)} fusion(f32[4,128,16384]{2,1,0:T(8,128)} %get-tuple-element.1026, s32[]{:T(128)} %get-tuple-element.1025, f32[128]{0:T(128)S(1)} %dynamic_slice.129, s32[16384]{0:T(1024)S(1)} %get-tuple-element.1048, s32[128]{0:T(128)S(1)} %dynamic_slice.130, s32[16384]{0:T(1024)S(1)} %get-tuple-element.1046, ...), kind=kLoop, calls=%fused_computation.17.clone.1 | loop fusion | flops 29360128 | bytes 8588288 | tf_op jit(solution)/shard_map/while/body/jit(dynamic_update_index_in_dim)/dynamic_update_slice | solution.py:72
  289.5 6.3 %fusion.35 = f32[4,128,16384]{2,1,0:T(8,128)} fusion(f32[4,128,16384]{2,1,0:T(8,128)} %get-tuple-element.1026, s32[]{:T(128)} %get-tuple-element.1025, f32[128]{0:T(128)S(1)} %dynamic_slice.129, s32[16384]{0:T(1024)S(1)} %get-tuple-element.1048, s32[128]{0:T(128)S(1)} %dynamic_slice.130, s32[16384]{0:T(1024)S(1)} %get-tuple-element.1046, ...), kind=kLoop, calls=%fused_computation.17.clone.1 | loop fusion | flops 29360128 | bytes 8588288 | tf_op jit(solution)/shard_map/while/body/jit(dynamic_update_index_in_dim)/dynamic_update_slice | solution.py:72
  299.2 6.2 %fusion.35 = f32[4,128,16384]{2,1,0:T(8,128)} fusion(f32[4,128,16384]{2,1,0:T(8,128)} %get-tuple-element.1026, s32[]{:T(128)} %get-tuple-element.1025, f32[128]{0:T(128)S(1)} %dynamic_slice.129, s32[16384]{0:T(1024)S(1)} %get-tuple-element.1048, s32[128]{0:T(128)S(1)} %dynamic_slice.130, s32[16384]{0:T(1024)S(1)} %get-tuple-element.1046, ...), kind=kLoop, calls=%fused_computation.17.clone.1 | loop fusion | flops 29360128 | bytes 8588288 | tf_op jit(solution)/shard_map/while/body/jit(dynamic_update_index_in_dim)/dynamic_update_slice | solution.py:72
  305.5 17.0 %all-gather.7.cloned.1.call-done = f32[16384,32]{0,1:T(8,128)} async-done(((f32[512,32]{0,1:T(8,128)}), f32[16384,32]{0,1:T(8,128)}) %all-gather.7.cloned.1.call-update) | async-done | bytes 2097168 | tf_op jit(solution)/shard_map/all_gather | solution.py:80
  322.4 35.0 %fusion.17 = f32[512,32]{0,1:T(8,128)} fusion(f32[512,16384]{1,0:T(8,128)} %bitcast.30, f32[16384,32]{0,1:T(8,128)} %all-gather.7.cloned.1.call-done, f32[512]{0:T(512)S(1)} %copy-done.4, s32[512]{0:T(512)S(1)} %add_select_fusion.2, s32[32]{0:T(128)S(1)} %copy-done.6), kind=kOutput, calls=%fused_computation.36 | convolution fusion | flops 3221274624 | bytes 35721344 | tf_op jit(solution)/shard_map/dot_general | solution.py:83
  357.5 55.3 %all-gather.9.cloned.1.call-done = f32[16384,32]{0,1:T(8,128)} async-done(((f32[512,32]{0,1:T(8,128)}), f32[16384,32]{0,1:T(8,128)}) %all-gather.9.cloned.1.call-update) | async-done | bytes 2097168 | tf_op jit(solution)/shard_map/all_gather | solution.py:80
  412.7 35.0 %fusion.16 = f32[512,32]{0,1:T(8,128)} fusion(f32[512,16384]{1,0:T(8,128)} %bitcast.31, f32[16384,32]{0,1:T(8,128)} %all-gather.9.cloned.1.call-done, f32[512]{0:T(512)S(1)} %copy-done.4, s32[512]{0:T(512)S(1)} %add_select_fusion.2, s32[32]{0:T(128)S(1)} %copy-done.6), kind=kOutput, calls=%fused_computation.34 | convolution fusion | flops 3221274624 | bytes 35721344 | tf_op jit(solution)/shard_map/dot_general | solution.py:83
  (149 shorter events, 13.8 us)
Async XLA Ops:
  7.2 133.5 %copy-start.3 = (f32[16384]{0:T(1024)S(1)}, f32[16384]{0:T(1024)}, u32[]{:S(2)}) copy-start(f32[16384]{0:T(1024)} %param.17) | copy-start | bytes 196612
  7.2 167.0 %copy-start.5 = (f32[512]{0:T(512)S(1)}, f32[512]{0:T(512)}, u32[]{:S(2)}) copy-start(f32[512]{0:T(512)} %param.16) | copy-start | bytes 6148
  7.2 167.0 %copy-start.7 = (f32[512]{0:T(512)S(1)}, f32[512]{0:T(512)}, u32[]{:S(2)}) copy-start(f32[512]{0:T(512)} %param.18) | copy-start | bytes 6148
  7.2 202.0 %copy-start.4 = (f32[512]{0:T(512)S(1)}, f32[512]{0:T(512)}, u32[]{:S(2)}) copy-start(f32[512]{0:T(512)} %param.19) | copy-start | bytes 6148
  7.2 202.0 %copy-start.6 = (s32[32]{0:T(128)S(1)}, s32[32]{0:T(128)}, u32[]{:S(2)}) copy-start(s32[32]{0:T(128)} %param.21) | copy-start | bytes 388
  7.2 131.5 %all-gather.11.cloned.1.call-start = ((), (), s32[]{:S(2)}) async-start(), calls=%async_computation.2 | async-start | bytes 2162688 | tf_op jit(solution)/shard_map/all_gather | solution.py:61
  78.9 0.6 copy-start.1
  79.5 185.0 %all-gather.13.cloned.1.call-start = ((), (), s32[]{:S(2)}) async-start(), calls=%async_computation.3 | async-start | bytes 2162688 | tf_op jit(solution)/shard_map/all_gather | solution.py:61
  208.5 0.6 copy-start.2
  209.1 113.3 %all-gather.7.cloned.1.call-start = ((), (), s32[]{:S(2)}) async-start(), calls=%async_computation | async-start | bytes 2162688 | tf_op jit(solution)/shard_map/all_gather | solution.py:80
  209.9 202.8 %all-gather.9.cloned.1.call-start = ((), (), s32[]{:S(2)}) async-start(), calls=%async_computation.1 | async-start | bytes 2162688 | tf_op jit(solution)/shard_map/all_gather | solution.py:80
  305.5 52.0 %copy-start = (f32[16384]{0:T(1024)}, f32[16384]{0:T(1024)S(1)}, u32[]{:S(2)}) copy-start(f32[16384]{0:T(1024)S(1)} %get-tuple-element.1067) | copy-start | bytes 196612
  305.5 52.0 %copy-start.8 = (f32[512]{0:T(512)}, f32[512]{0:T(512)S(1)}, u32[]{:S(2)}) copy-start(f32[512]{0:T(512)S(1)} %get-tuple-element.1081) | copy-start | bytes 6148
Sparse Core Ops, SparseCore 0:
  79.6 59.0 all-gather.10
  209.3 55.2 all-gather.12
  267.4 54.9 all-gather.6
  357.6 55.1 all-gather.8
